TPU v7x, 512 devices: a whole 4x8x8 slice. The times are simulated.
512 devices in a mesh: replica: 64 (over x, z, y_lo), tensor: 8 (over y_hi, core).
Axes of the slice: x: 4, y: 8 (y_hi: 4, y_lo: 2; y = y_hi * 2 + y_lo), z: 8, core: 2. Of those that a mesh axis runs over, the one named last changes fastest.
Arguments:
- global_start: bfloat16 [256, 8192], P(None, 'tensor'), may hold values from -6 to 6
- local_params: bfloat16 [64, 2, 256, 8192], P('replica', None, None, 'tensor'), may hold values from -16 to 16
- layer_index: int32 [64], P('replica'), may hold values from 0 to 1
- momentum: float32 [256, 8192], P('replica', 'tensor'), may hold values from -6 to 6
- queries: bfloat16 [64, 1024, 4096], P('replica', None, 'tensor'), may hold values from -6 to 6
- keyvals: bfloat16 [64, 2, 1024, 1024], P('replica', None, None, 'tensor'), may hold values from -6 to 6
- segment_ids: int32 [64, 1024], P('replica'), may hold values from 0 to 3, never falling along the last dimension, each value on 1 to 512 neighbouring positions
Outputs:
- new_momentum: float32 [256, 8192], P('replica', 'tensor')
- blended: bfloat16 [64, 256, 8192], P('replica', None, 'tensor')
- attended: bfloat16 [64, 1024, 4096], P('replica', None, 'tensor')
All inputs are finite; a program needn't handle non-finite values.
Results may differ from a plain program's by a relative error of at most 0.009.
Values may be sent and summed in bfloat16 or wider, within the bound.
A program may use at most 64 MiB of HBM per device.

v0:
```python
import jax
import jax.numpy as jnp
from jax import lax
from jax.sharding import PartitionSpec as P

D = 8192
FRAG = 256


def attend_local(query, keys, values, segment):
    length = query.shape[0]
    block = min(512, length)
    size = keys.shape[1]
    heads = query.shape[1] // size
    qblocks = query.reshape(length // block, block, heads, size)
    positions = jnp.arange(length, dtype=jnp.int32)
    starts = jnp.arange(length // block, dtype=jnp.int32) * block

    def one_block(args):
        qblock, first = args
        rows = first + jnp.arange(block, dtype=jnp.int32)
        rowseg = lax.dynamic_slice_in_dim(segment, first, block, 0)
        allowed = (rowseg[:, None] == segment[None, :]) & (positions[None, :] <= rows[:, None])
        scores = jnp.einsum(
            "bhd,kd->hbk", qblock, keys, preferred_element_type=jnp.float32
        ) / jnp.sqrt(jnp.float32(size))
        scores = jnp.where(allowed[None], scores, jnp.float32(-1e30))
        peak = jnp.max(scores, axis=-1, keepdims=True)
        expo = jnp.exp(scores - peak)
        probs = (expo / jnp.sum(expo, axis=-1, keepdims=True)).astype(jnp.bfloat16)
        out = jnp.einsum("hbk,kd->bhd", probs, values, preferred_element_type=jnp.float32)
        return out.astype(jnp.bfloat16).reshape(block, heads * size)

    return lax.map(one_block, (qblocks, starts)).reshape(length, heads * size)


def shards(global_start, local_params, layer_index, momentum, queries, keyvals, segment_ids):
    replicas = lax.axis_size("replica")
    layer = lax.dynamic_index_in_dim(local_params[0], layer_index[0], 0, keepdims=False)
    start_full = global_start.astype(jnp.float32)
    delta = start_full - layer.astype(jnp.float32)
    count = jnp.float32(FRAG * D)
    owned = momentum.shape[0]
    total = lax.psum(delta, "replica")
    average = total / replicas
    square = lax.psum(jnp.sum(average * average), "tensor")
    grad = average * lax.rsqrt(square / count + 1e-06)
    all_momentum = lax.all_gather(momentum, "replica", axis=0, tiled=True)
    moment_full = 0.9 * all_momentum + grad
    new_global = (start_full - 0.7 * (grad + 0.9 * moment_full)).astype(jnp.bfloat16)
    first = lax.axis_index("replica") * owned
    new_momentum = lax.dynamic_slice_in_dim(moment_full, first, owned, 0)
    blended = (0.5 * layer.astype(jnp.float32) + 0.5 * new_global.astype(jnp.float32)).astype(
        jnp.bfloat16
    )
    attended = attend_local(queries[0], keyvals[0, 0], keyvals[0, 1], segment_ids[0])
    return (new_momentum, blended[None], attended[None])


def solution(mesh):
    in_specs = (
        P(None, "tensor"),
        P("replica", None, None, "tensor"),
        P("replica"),
        P("replica", "tensor"),
        P("replica", None, "tensor"),
        P("replica", None, None, "tensor"),
        P("replica", None),
    )
    out_specs = (P("replica", "tensor"), P("replica", None, "tensor"), P("replica", None, "tensor"))
    return jax.shard_map(shards, mesh=mesh, in_specs=in_specs, out_specs=out_specs, check_vma=False)
```

profile of v0, /device:TPU:16, one launch (start us, length us, event | category | flops | bytes accessed | tf_op | source)
XLA Modules:
  0.0 937.3 jit_solution(3532674147950996421)
XLA Ops:
  7.2 0.0 all-reduce.2.cloned.1.call-start
  7.9 2.4 convert_subtract_fusion
  10.2 0.0 all-reduce.2.cloned.1.call-update
  10.2 0.0 all-gather.3.cloned.1.call-start
  10.3 0.7 all-gather.3.cloned.1.call-update
  11.0 1.1 fusion.32
  12.1 0.1 copy.21
  12.2 1.3 reshape_squeeze.3
  13.6 0.0 copy-start
  13.6 33.7 %while.11 = (s32[]{:T(128)}, bf16[2,512,512]{2,1,0:T(8,128)(2,1)}, s32[2]{0:T(128)S(1)}, s32[1024]{0:T(1024)}, s32[1,1024]{1,0:T(1,128)}, /*index=5*/bf16[2,512,...) while((s32[]{:T(128)}, bf16[2,512,512]{2,1,0:T(8,128)(2,1)}, ...), condition=%wide.region_6.7_spmd.clone, body=%wide.region_3.6_spmd.clone.sunk | while | flops 1088161280 | bytes 22575784 | solution.py:34
  13.6 0.6 dynamic_slice.31
  16.1 0.8 dynamic_slice.32
  16.9 0.6 iota_add_fusion.2
  17.6 1.3 fusion.40
  18.8 0.2 constant_dynamic-slice_fusion.3
  19.0 5.4 fusion.41
  24.4 5.0 fusion.42
  29.4 0.2 copy.36
  29.6 0.8 constant_dynamic-update-slice_fusion.2
  30.4 0.6 dynamic_slice.31
  33.0 0.8 dynamic_slice.32
  33.7 0.6 iota_add_fusion.2
  34.4 1.3 fusion.40
  35.7 0.2 constant_dynamic-slice_fusion.3
  35.9 5.4 fusion.41
  41.2 5.0 fusion.42
  46.2 0.2 copy.36
  46.4 0.8 constant_dynamic-update-slice_fusion.2
  47.3 579.2 %all-reduce.2.cloned.1.call-done = f32[256,1024]{1,0:T(8,128)} async-done(((f32[256,1024]{1,0:T(8,128)}), f32[256,1024]{1,0:T(8,128)}) %all-reduce.2.cloned.1.call-update) | async-done | bytes 1048592 | tf_op jit(solution)/shard_map/psum | solution.py:44
  626.5 2.1 multiply_reduce_fusion
  628.6 12.7 %psum.15 = f32[]{:T(128)} all-reduce(f32[]{:T(128)} %multiply_reduce_fusion), channel_id=1, replica_groups=mesh['replica'=64,'tensor'=8] {'tensor'}, use_global_device_ids=true, to_apply=%region_2.3 | all-reduce | flops 1 | bytes 8 | tf_op jit(solution)/shard_map/psum | solution.py:46
  642.0 283.4 %all-gather.3.cloned.1.call-done = f32[64,4,1024]{2,1,0:T(4,128)} async-done(((f32[1,4,1024]{2,1,0:T(4,128)}), f32[64,4,1024]{2,1,0:T(4,128)}) %all-gather.3.cloned.1.call-update) | async-done | bytes 1048592 | tf_op jit(solution)/shard_map/all_gather | solution.py:48
  925.4 1.6 broadcast_multiply_fusion
  926.9 0.4 reshape.79
  927.3 0.0 copy-done
  927.3 2.6 fusion.26
  929.8 0.6 constant_dynamic-slice_fusion.1
  (2 shorter events, 0.0 us)
Async XLA Ops:
  7.2 619.3 %all-reduce.2.cloned.1.call-start = ((), (), s32[]{:S(2)}) async-start(), calls=%async_computation | async-start | bytes 2097152 | tf_op jit(solution)/shard_map/psum | solution.py:44
  10.2 915.1 %all-gather.3.cloned.1.call-start = ((), (), s32[]{:S(2)}) async-start(), calls=%async_computation.1 | async-start | bytes 1064960 | tf_op jit(solution)/shard_map/all_gather | solution.py:48
  13.6 913.7 %copy-start = (bf16[256,1024]{1,0:T(8,128)(2,1)S(1)}, bf16[256,1024]{1,0:T(8,128)(2,1)}, u32[]{:S(2)}) copy-start(bf16[256,1024]{1,0:T(8,128)(2,1)} %param.9) | copy-start | bytes 1572868
Sparse Core Ops, SparseCore 0:
  10.9 615.5 all-reduce.1
  628.8 296.5 all-gather.2
where the time goes:
time: 938 us; the launch traced here: 937 us
  waiting for transfers between devices  863 us (92%)
  matrix products  20.7 us (2%)
  between operations  15.4 us (2%)
  blocking collectives  12.7 us (1%)
  other arithmetic  12.4 us (1%)
    psum x1, waiting for transfers between devices, shards(): total = lax.psum(delta, 'replica')  579 us
    all_gather x1, waiting for transfers between devices, shards(): all_momentum = lax.all_gather(momentum, 'replica', axis=0, tiled=True)  283 us
  transfers between devices with their start and end apart: 2, of which 2 were waited for; matrix products, arithmetic and copies ran while one was open for 4% of the time, Pallas kernels for 0%

commit v1 on v0

v1 whole, which is shorter than its diff:
```python
import jax
import jax.numpy as jnp
from jax import lax
from jax.experimental import pallas as pl
from jax.experimental.pallas import tpu as pltpu
from jax.sharding import PartitionSpec as P

D = 8192
FRAG = 256
REPLICAS = 64
MESH = pl.DeviceIdType.MESH
ROWS = 16
GROUP = 16
TWINS = 4
TENSOR = 8
BLOCK = 256
HEAD = 128
SPAN = 512
F32 = jnp.float32
BF16 = jnp.bfloat16


def fused(
    start_hbm, params_hbm, slot_ref, moment_hbm, query_hbm, keyval_hbm, segment_hbm,
    newmom_ref, blended_ref, attended_ref,
    start, params, layer, moment, query, keyval, segment, values, bias,
    reduce_buf, twin_buf, average, mom_twin, mom_all, mom_full, piece, sum_one, sum_two,
    local_sem, reduce_s, reduce_r, twin_s, twin_r, gather_s, gather_r,
    momone_s, momone_r, momtwo_s, momtwo_r, sumone_s, sumone_r, sumtwo_s, sumtwo_r,
):
    replica = lax.axis_index("replica")
    tensor = lax.axis_index("tensor")
    xs, twin, low = replica // 16, (replica // 4) % TWINS, replica % 4
    mine = xs * 4 + low

    def member(g):
        return ((g // 4) * 16 + twin * 4 + g % 4, tensor)

    def twin_of(t):
        return (xs * 16 + t * 4 + low, tensor)

    def rows_of(g):
        return pl.ds(pl.multiple_of(g * ROWS, ROWS), ROWS)

    def remote(src, dst, send, recv, device):
        return pltpu.make_async_remote_copy(
            src_ref=src, dst_ref=dst, send_sem=send, recv_sem=recv,
            device_id=device, device_id_type=MESH,
        )

    def reduce_copy(k):
        to = (mine + k) % GROUP
        return remote(layer.at[rows_of(to)], reduce_buf.at[mine], reduce_s.at[k], reduce_r.at[mine], member(to))

    def twin_copy(k):
        return remote(twin_buf.at[twin], twin_buf.at[twin], twin_s.at[k], twin_r.at[twin], twin_of((twin + k) % TWINS))

    def gather_copy(k):
        return remote(average.at[mine], average.at[mine], gather_s.at[k], gather_r.at[mine], member((mine + k) % GROUP))

    def momone_copy(k):
        return remote(moment, mom_twin.at[twin], momone_s.at[k], momone_r.at[twin], twin_of((twin + k) % TWINS))

    def momtwo_copy(k):
        return remote(mom_all.at[mine], mom_all.at[mine], momtwo_s.at[k], momtwo_r.at[mine], member((mine + k) % GROUP))

    def sumone_copy(k):
        return remote(
            sum_one.at[tensor], sum_one.at[tensor], sumone_s.at[k], sumone_r.at[tensor],
            (replica, (tensor + k) % TENSOR),
        )

    def sumtwo_copy(k):
        return remote(sum_two.at[mine], sum_two.at[mine], sumtwo_s.at[k], sumtwo_r.at[mine], member((mine + k) % GROUP))

    def each(count, act):
        def step(k, carry):
            act(k)
            return carry
        lax.fori_loop(1, count, step, 0, unroll=True)

    def arrived(slots, sems, slot):
        pltpu.make_async_copy(slots.at[slot], slots.at[slot], sems.at[slot]).wait()

    loads = [
        pltpu.make_async_copy(params_hbm.at[0], params, local_sem.at[0]),
        pltpu.make_async_copy(start_hbm, start, local_sem.at[1]),
        pltpu.make_async_copy(moment_hbm, moment, local_sem.at[2]),
        pltpu.make_async_copy(keyval_hbm.at[0], keyval, local_sem.at[3]),
        pltpu.make_async_copy(segment_hbm, segment, local_sem.at[4]),
        pltpu.make_async_copy(query_hbm.at[0], query, local_sem.at[5]),
    ]
    for load in loads:
        load.start()

    barrier = pltpu.get_barrier_semaphore()

    def greet(device):
        pl.semaphore_signal(barrier, inc=1, device_id=device, device_id_type=MESH)

    each(GROUP, lambda k: greet(member((mine + k) % GROUP)))
    each(TWINS, lambda k: greet(twin_of((twin + k) % TWINS)))
    each(TENSOR, lambda k: greet((replica, (tensor + k) % TENSOR)))

    loads[0].wait()
    slot = slot_ref[0]
    layer[...] = params[slot]
    loads[2].wait()
    pl.semaphore_wait(barrier, GROUP + TWINS + TENSOR - 3)

    each(GROUP, lambda k: reduce_copy(k).start())
    each(TWINS, lambda k: momone_copy(k).start())

    loads[3].wait()
    loads[4].wait()
    loads[5].wait()
    values[:, :HEAD] = keyval[1]
    values[:, HEAD:] = jnp.ones((values.shape[0], HEAD), BF16)
    scale = 1.4426950408889634 / (HEAD ** 0.5)

    def attend(block):
        first, last = block * BLOCK, (block + 1) * BLOCK
        begin = max(0, first - SPAN)
        width = last - begin
        own = jnp.broadcast_to(segment[:, first:last], (BLOCK, BLOCK)).T
        for at in range(begin, last, BLOCK):
            keep = own == segment[:, at:at + BLOCK]
            if at == first:
                row = lax.broadcasted_iota(jnp.int32, (BLOCK, BLOCK), 0)
                col = lax.broadcasted_iota(jnp.int32, (BLOCK, BLOCK), 1)
                keep = keep & (col <= row)
            bias[:, at - begin:at - begin + BLOCK] = jnp.where(keep, 0.0, -1e30).astype(F32)

        def head(h, carry):
            columns = pl.ds(pl.multiple_of(h * HEAD, HEAD), HEAD)
            scores = lax.dot_general(
                query[first:last, columns], keyval[0, begin:last, :],
                (((1,), (1,)), ((), ())), preferred_element_type=F32,
            )
            scores = scores * scale + bias[:, :width]
            peak = jnp.max(scores, axis=1, keepdims=True)
            expo = jnp.exp2(scores - peak).astype(BF16)
            out = jnp.dot(expo, values[begin:last, :], preferred_element_type=F32)
            attended_ref[0, first:last, columns] = (out[:, :HEAD] / out[:, HEAD:]).astype(BF16)
            return carry

        lax.fori_loop(0, query.shape[1] // HEAD, head, 0)

    attend(3)
    attend(2)

    loads[1].wait()
    base = start[rows_of(mine), :].astype(F32)

    def add(k, total):
        place = (mine - k + GROUP) % GROUP
        arrived(reduce_buf, reduce_r, place)
        return total + (base - reduce_buf[place].astype(F32))

    partial = lax.fori_loop(1, GROUP, add, base - layer[rows_of(mine), :].astype(F32), unroll=True)
    twin_buf[twin] = partial.astype(BF16)
    each(TWINS, lambda k: twin_copy(k).start())

    mom_twin[twin] = moment[...]
    each(TWINS, lambda k: arrived(mom_twin, momone_r, (twin + k) % TWINS))
    for t in range(TWINS):
        piece[4 * t:4 * t + 4, :] = mom_twin[t]
    mom_all[mine] = piece[...].astype(BF16)
    each(GROUP, lambda k: momtwo_copy(k).start())

    attend(1)
    attend(0)

    each(TWINS, lambda k: arrived(twin_buf, twin_r, (twin + k) % TWINS))
    total = twin_buf[0].astype(F32)
    for t in range(1, TWINS):
        total = total + twin_buf[t].astype(F32)
    total = total * (1.0 / REPLICAS)
    average[mine] = total.astype(BF16)
    square = total * total
    parts = square[0:8, 0:128]
    for r in range(0, ROWS, 8):
        for c in range(0, square.shape[1], 128):
            if r or c:
                parts = parts + square[r:r + 8, c:c + 128]
    sum_one[tensor] = parts
    each(TENSOR, lambda k: sumone_copy(k).start())
    each(GROUP, lambda k: gather_copy(k).start())

    each(TENSOR, lambda k: arrived(sum_one, sumone_r, (tensor + k) % TENSOR))
    parts = sum_one[0]
    for t in range(1, TENSOR):
        parts = parts + sum_one[t]
    sum_two[mine] = parts
    each(GROUP, lambda k: sumtwo_copy(k).start())

    each(GROUP, lambda k: arrived(mom_all, momtwo_r, (mine - k + GROUP) % GROUP))
    for g in range(GROUP):
        piece[...] = mom_all[g].astype(F32)
        for t in range(TWINS):
            at = (g // 4) * 64 + t * 16 + (g % 4) * 4
            mom_full[at:at + 4, :] = piece[4 * t:4 * t + 4, :]

    each(GROUP, lambda k: arrived(average, gather_r, (mine - k + GROUP) % GROUP))
    each(GROUP, lambda k: arrived(sum_two, sumtwo_r, (mine - k + GROUP) % GROUP))
    parts = sum_two[0]
    for g in range(1, GROUP):
        parts = parts + sum_two[g]
    square = jnp.sum(jnp.sum(parts, axis=1, keepdims=True), axis=0, keepdims=True)
    factor = lax.rsqrt(square * (1.0 / (FRAG * D)) + 1e-06)

    def update(c, carry):
        rows = rows_of(c)
        grad = average[c].astype(F32) * factor
        moved = 0.9 * mom_full[rows, :] + grad
        fresh = (start[rows, :].astype(F32) - 0.7 * (grad + 0.9 * moved)).astype(BF16)
        blended_ref[0, rows, :] = (0.5 * layer[rows, :].astype(F32) + 0.5 * fresh.astype(F32)).astype(BF16)
        return carry

    lax.fori_loop(0, GROUP, update, 0)

    piece[...] = average[replica // 4].astype(F32)
    own = piece[0:4, :]
    for t in range(1, 4):
        own = jnp.where(low == t, piece[4 * t:4 * t + 4, :], own)
    newmom_ref[...] = 0.9 * moment[...] + own * factor

    each(GROUP, lambda k: reduce_copy(k).wait_send())
    each(TWINS, lambda k: twin_copy(k).wait_send())
    each(GROUP, lambda k: gather_copy(k).wait_send())
    each(TWINS, lambda k: momone_copy(k).wait_send())
    each(GROUP, lambda k: momtwo_copy(k).wait_send())
    each(TENSOR, lambda k: sumone_copy(k).wait_send())
    each(GROUP, lambda k: sumtwo_copy(k).wait_send())


def shards(global_start, local_params, layer_index, momentum, queries, keyvals, segment_ids):
    rows, columns = global_start.shape
    length, width = queries.shape[1:]
    whole = pl.BlockSpec(memory_space=pltpu.VMEM)
    far = pl.BlockSpec(memory_space=pl.ANY)
    dma = pltpu.SemaphoreType.DMA
    return pl.pallas_call(
        fused,
        out_shape=(
            jax.ShapeDtypeStruct(momentum.shape, F32),
            jax.ShapeDtypeStruct((1, rows, columns), BF16),
            jax.ShapeDtypeStruct(queries.shape, BF16),
        ),
        in_specs=[far, far, pl.BlockSpec(memory_space=pltpu.SMEM), far, far, far, far],
        out_specs=(whole, whole, whole),
        scratch_shapes=[
            pltpu.VMEM((rows, columns), BF16),
            pltpu.VMEM(local_params.shape[1:], BF16),
            pltpu.VMEM((rows, columns), BF16),
            pltpu.VMEM(momentum.shape, F32),
            pltpu.VMEM((length, width), BF16),
            pltpu.VMEM(keyvals.shape[1:], BF16),
            pltpu.VMEM((1, length), jnp.int32),
            pltpu.VMEM((length, 2 * HEAD), BF16),
            pltpu.VMEM((BLOCK, BLOCK + SPAN), F32),
            pltpu.VMEM((GROUP, ROWS, columns), BF16),
            pltpu.VMEM((TWINS, ROWS, columns), BF16),
            pltpu.VMEM((GROUP, ROWS, columns), BF16),
            pltpu.VMEM((TWINS, 4, columns), F32),
            pltpu.VMEM((GROUP, ROWS, columns), BF16),
            pltpu.VMEM((rows, columns), F32),
            pltpu.VMEM((ROWS, columns), F32),
            pltpu.VMEM((TENSOR, 8, 128), F32),
            pltpu.VMEM((GROUP, 8, 128), F32),
            dma((6,)),
            dma((GROUP,)), dma((GROUP,)),
            dma((TWINS,)), dma((TWINS,)),
            dma((GROUP,)), dma((GROUP,)),
            dma((TWINS,)), dma((TWINS,)),
            dma((GROUP,)), dma((GROUP,)),
            dma((TENSOR,)), dma((TENSOR,)),
            dma((GROUP,)), dma((GROUP,)),
        ],
        compiler_params=pltpu.CompilerParams(
            collective_id=0, has_side_effects=True, vmem_limit_bytes=48 * 1024 * 1024
        ),
    )(global_start, local_params, layer_index, momentum, queries, keyvals, segment_ids)


def solution(mesh):
    in_specs = (
        P(None, "tensor"),
        P("replica", None, None, "tensor"),
        P("replica"),
        P("replica", "tensor"),
        P("replica", None, "tensor"),
        P("replica", None, None, "tensor"),
        P("replica", None),
    )
    out_specs = (P("replica", "tensor"), P("replica", None, "tensor"), P("replica", None, "tensor"))
    return jax.shard_map(shards, mesh=mesh, in_specs=in_specs, out_specs=out_specs, check_vma=False)
```

time: 938 us -> 53.5 us (0.06)
  the two profiles are of different devices: /device:TPU:16 before, /device:TPU:8 now
where the time goes in v1:
time: 53.5 us; the launch traced here: 53.1 us
  Pallas kernels  43.5 us (81%)
  local copies, waits for them, and re-layouts  8.3 us (16%)
  between operations  1.3 us (2%)
    pallas_call x1, Pallas kernels, shards(): pl.pallas_call(fused, out_shape=(jax.ShapeDtypeStruct(momentum.shape, F32...  43.5 us
    unnamed x15, local copies, waits for them, and re-layouts  8.3 us

profile of v1, /device:TPU:8, one launch (start us, length us, event | category | flops | bytes accessed | tf_op | source)
XLA Modules:
  0.0 53.1 jit_solution(2546503512346114388)
XLA Ops:
  1.3 0.0 copy-start
  1.3 1.2 %copy-done = bf16[1,2,256,1024]{3,2,1,0:T(8,128)(2,1)S(1)} copy-done((bf16[1,2,256,1024]{3,2,1,0:T(8,128)(2,1)S(1)}, bf16[1,2,256,1024]{3,2,1,0:T(8,128)(2,1)}, u32[]{:S(2)}) %copy-start) | copy-done | bytes 1048600
  2.5 0.0 copy-start.1
  2.5 1.2 %copy-done.1 = bf16[1,1024,512]{2,1,0:T(8,128)(2,1)S(1)} copy-done((bf16[1,1024,512]{2,1,0:T(8,128)(2,1)S(1)}, bf16[1,1024,512]{2,1,0:T(8,128)(2,1)}, u32[]{:S(2)}) %copy-start.1) | copy-done | bytes 1048600
  3.7 0.0 copy-start.2
  3.7 1.0 %copy-done.2 = bf16[256,1024]{1,0:T(8,128)(2,1)S(1)} copy-done((bf16[256,1024]{1,0:T(8,128)(2,1)S(1)}, bf16[256,1024]{1,0:T(8,128)(2,1)}, u32[]{:S(2)}) %copy-start.2) | copy-done | bytes 524312
  4.8 0.0 copy-start.3
  4.8 1.0 %copy-done.3 = bf16[1,2,1024,128]{3,2,1,0:T(8,128)(2,1)S(1)} copy-done((bf16[1,2,1024,128]{3,2,1,0:T(8,128)(2,1)S(1)}, bf16[1,2,1024,128]{3,2,1,0:T(8,128)(2,1)}, u32[]{:S(2)}) %copy-start.3) | copy-done | bytes 524312
  5.8 0.0 copy-start.4
  5.8 0.7 %copy-done.4 = f32[4,1024]{1,0:T(4,128)S(1)} copy-done((f32[4,1024]{1,0:T(4,128)S(1)}, f32[4,1024]{1,0:T(4,128)}, u32[]{:S(2)}) %copy-start.4) | copy-done | bytes 16408
  6.5 0.0 copy-start.5
  6.5 0.7 %copy-done.5 = s32[1,1024]{1,0:T(1,128)S(1)} copy-done((s32[1,1024]{1,0:T(1,128)S(1)}, s32[1,1024]{1,0:T(1,128)}, u32[]{:S(2)}) %copy-start.5) | copy-done | bytes 4120
  7.2 43.5 %shard_map.94 = (f32[4,1024]{1,0:T(4,128)S(1)}, bf16[1,256,1024]{2,1,0:T(8,128)(2,1)S(1)}, bf16[1,1024,512]{2,1,0:T(8,128)(2,1)S(1)}) custom-call(bf16[256,1024]{1,0:T(8,128)(2,1)S(1)} %copy-done.2, bf16[1,2,256,1024]{3,2,1,0:T(8,128)(2,1)S(1)} %copy-done, s32[1]{0:T(128)S(6)} %copy.13.slot_ref, f32[4,1024]{1,0:T(4,128)S(1)} %copy-done.4, ...), custom_call_target="tpu_custom_call" | custom-call | tf_op jit(solution)/shard_map/pallas_call | solution.py:243
  50.8 0.6 %copy.14 = f32[4,1024]{1,0:T(4,128)} copy(f32[4,1024]{1,0:T(4,128)S(1)} %get-tuple-element.6) | data formatting | bytes 32768
  51.4 0.8 %copy.15 = bf16[1,256,1024]{2,1,0:T(8,128)(2,1)} copy(bf16[1,256,1024]{2,1,0:T(8,128)(2,1)S(1)} %get-tuple-element.7) | data formatting | bytes 1048576
  52.2 1.0 %copy.16 = bf16[1,1024,512]{2,1,0:T(8,128)(2,1)} copy(bf16[1,1024,512]{2,1,0:T(8,128)(2,1)S(1)} %get-tuple-element.8) | data formatting | bytes 2097152
Async XLA Ops:
  1.3 1.2 %copy-start = (bf16[1,2,256,1024]{3,2,1,0:T(8,128)(2,1)S(1)}, bf16[1,2,256,1024]{3,2,1,0:T(8,128)(2,1)}, u32[]{:S(2)}) copy-start(bf16[1,2,256,1024]{3,2,1,0:T(8,128)(2,1)} %params_hbm.1) | copy-start | bytes 3145732
  2.5 1.2 %copy-start.1 = (bf16[1,1024,512]{2,1,0:T(8,128)(2,1)S(1)}, bf16[1,1024,512]{2,1,0:T(8,128)(2,1)}, u32[]{:S(2)}) copy-start(bf16[1,1024,512]{2,1,0:T(8,128)(2,1)} %query_hbm.1) | copy-start | bytes 3145732
  3.7 1.0 %copy-start.2 = (bf16[256,1024]{1,0:T(8,128)(2,1)S(1)}, bf16[256,1024]{1,0:T(8,128)(2,1)}, u32[]{:S(2)}) copy-start(bf16[256,1024]{1,0:T(8,128)(2,1)} %start_hbm.1) | copy-start | bytes 1572868
  4.8 1.0 %copy-start.3 = (bf16[1,2,1024,128]{3,2,1,0:T(8,128)(2,1)S(1)}, bf16[1,2,1024,128]{3,2,1,0:T(8,128)(2,1)}, u32[]{:S(2)}) copy-start(bf16[1,2,1024,128]{3,2,1,0:T(8,128)(2,1)} %keyval_hbm.1) | copy-start | bytes 1572868
  5.8 0.7 %copy-start.4 = (f32[4,1024]{1,0:T(4,128)S(1)}, f32[4,1024]{1,0:T(4,128)}, u32[]{:S(2)}) copy-start(f32[4,1024]{1,0:T(4,128)} %moment_hbm.1) | copy-start | bytes 49156
  6.5 0.7 %copy-start.5 = (s32[1,1024]{1,0:T(1,128)S(1)}, s32[1,1024]{1,0:T(1,128)}, u32[]{:S(2)}) copy-start(s32[1,1024]{1,0:T(1,128)} %segment_hbm.1) | copy-start | bytes 12292

commit v2 on v1

v2 whole, which is shorter than its diff:
```python
import jax
import jax.numpy as jnp
from jax import lax
from jax.experimental import pallas as pl
from jax.experimental.pallas import tpu as pltpu
from jax.sharding import PartitionSpec as P

D = 8192
FRAG = 256
REPLICAS = 64
MESH = pl.DeviceIdType.MESH
ROWS = 16
GROUP = 16
TWINS = 4
PLANE = 16
LINE = 8
COLUMN = 8
SHEET = 8
BLOCK = 256
HEAD = 128
SPAN = 512
F32 = jnp.float32
BF16 = jnp.bfloat16


def fused(
    start_hbm, params_hbm, slot_hbm, moment_hbm, query_hbm, keyval_hbm, segment_hbm,
    newmom_hbm, blended_hbm, attended_hbm,
    newmom, blended, attended, slot_ref, start, params, layer, moment, query, keyval, segment, values, bias,
    reduce_buf, twin_buf, average, mom_all, mom_full, piece, sum_one, sum_two,
    local_sem, reduce_s, reduce_r, twin_s, twin_r, gather_s, gather_r,
    momone_s, momone_r, momtwo_s, momtwo_r, sumone_s, sumone_r, sumtwo_s, sumtwo_r,
):
    replica = lax.axis_index("replica")
    tensor = lax.axis_index("tensor")
    xs, twin, low = replica // 16, (replica // 4) % TWINS, replica % 4
    mine = xs * 4 + low
    plane = (replica // 16) * 4 + ((replica // 2) % 2) * 2 + tensor % 2
    line = (tensor // 2) * 2 + replica % 2
    column = (replica // 2) % COLUMN
    sheet = xs * 2 + replica % 2

    def member(g):
        return ((g // 4) * 16 + twin * 4 + g % 4, tensor)

    def twin_of(t):
        return (xs * 16 + t * 4 + low, tensor)

    def plane_of(p):
        return ((p // 4) * 16 + twin * 4 + ((p // 2) % 2) * 2 + replica % 2, (tensor // 2) * 2 + p % 2)

    def line_of(y):
        return ((replica // 2) * 2 + y % 2, (y // 2) * 2 + tensor % 2)

    def column_of(z):
        return (xs * 16 + z * 2 + replica % 2, tensor)

    def sheet_of(p):
        return ((p // 2) * 16 + column * 2 + p % 2, tensor)

    def rows_of(g):
        return pl.ds(pl.multiple_of(g * ROWS, ROWS), ROWS)

    def remote(src, dst, send, recv, device):
        return pltpu.make_async_remote_copy(
            src_ref=src, dst_ref=dst, send_sem=send, recv_sem=recv,
            device_id=device, device_id_type=MESH,
        )

    def reduce_copy(k):
        to = (mine + k) % GROUP
        return remote(layer.at[rows_of(to)], reduce_buf.at[mine], reduce_s.at[k], reduce_r.at[mine], member(to))

    def twin_copy(k):
        return remote(twin_buf.at[twin], twin_buf.at[twin], twin_s.at[k], twin_r.at[twin], twin_of((twin + k) % TWINS))

    def gather_copy(k):
        return remote(average.at[mine], average.at[mine], gather_s.at[k], gather_r.at[mine], member((mine + k) % GROUP))

    def momone_copy(k):
        return remote(
            mom_all.at[sheet, column], mom_all.at[sheet, column], momone_s.at[k], momone_r.at[column],
            column_of((column + k) % COLUMN),
        )

    def momtwo_copy(k):
        return remote(
            mom_all.at[sheet], mom_all.at[sheet], momtwo_s.at[k], momtwo_r.at[sheet], sheet_of((sheet + k) % SHEET)
        )

    def sumone_copy(k):
        return remote(
            sum_one.at[plane], sum_one.at[plane], sumone_s.at[k], sumone_r.at[plane], plane_of((plane + k) % PLANE)
        )

    def sumtwo_copy(k):
        return remote(
            sum_two.at[line], sum_two.at[line], sumtwo_s.at[k], sumtwo_r.at[line], line_of((line + k) % LINE)
        )

    def each(count, act):
        def step(k, carry):
            act(k)
            return carry
        lax.fori_loop(1, count, step, 0, unroll=True)

    def arrived(slots, sems, slot):
        pltpu.make_async_copy(slots.at[slot], slots.at[slot], sems.at[slot]).wait()

    loads = [
        pltpu.make_async_copy(params_hbm.at[0], params, local_sem.at[0]),
        pltpu.make_async_copy(moment_hbm, moment, local_sem.at[1]),
        pltpu.make_async_copy(start_hbm, start, local_sem.at[2]),
        pltpu.make_async_copy(segment_hbm, segment, local_sem.at[3]),
        pltpu.make_async_copy(keyval_hbm.at[0], keyval, local_sem.at[4]),
        pltpu.make_async_copy(query_hbm.at[0], query, local_sem.at[5]),
    ]
    loads[0].start()
    index = pltpu.make_async_copy(slot_hbm, slot_ref, local_sem.at[10])
    index.start()

    barrier = pltpu.get_barrier_semaphore()

    def greet(device):
        pl.semaphore_signal(barrier, inc=1, device_id=device, device_id_type=MESH)

    each(GROUP, lambda k: greet(member((mine + k) % GROUP)))
    each(COLUMN // 2, lambda k: greet(column_of((column + 2 * k) % COLUMN)))
    each(COLUMN // 2, lambda k: greet(column_of((column + 2 * k) % COLUMN // 2 * 2 + 1 - column % 2)))
    for p in range(0, PLANE, 2):
        greet(plane_of(p + 1 - tensor % 2))
    each(LINE // 2, lambda k: greet(line_of((line + 2 * k) % LINE)))
    each(LINE // 2, lambda k: greet(line_of((line + 2 * k) % LINE // 2 * 2 + 1 - line % 2)))
    for load in loads[1:]:
        load.start()

    loads[0].wait()
    index.wait()
    slot = slot_ref[0]
    layer[...] = params[slot]
    loads[1].wait()
    fold = moment.shape[1] // 4
    for j in range(4):
        piece[4 * j:4 * j + 4, :fold] = moment[:, j * fold:(j + 1) * fold]
    mom_all[sheet, column] = piece[:, :fold].astype(BF16)
    pl.semaphore_wait(barrier, GROUP + COLUMN + PLANE // 2 + LINE - 5)

    each(COLUMN, lambda k: momone_copy(k).start())

    each(GROUP, lambda k: reduce_copy(k).start())
    for load in loads[3:]:
        load.wait()
    values[:, :HEAD] = keyval[1]
    values[:, HEAD:] = jnp.ones((values.shape[0], HEAD), BF16)
    scale = 1.4426950408889634 / (HEAD ** 0.5)

    def attend(block):
        first, last = block * BLOCK, (block + 1) * BLOCK
        begin = max(0, first - SPAN)
        width = last - begin
        own = jnp.broadcast_to(segment[:, first:last], (BLOCK, BLOCK)).T
        for at in range(begin, last, BLOCK):
            keep = own == segment[:, at:at + BLOCK]
            if at == first:
                row = lax.broadcasted_iota(jnp.int32, (BLOCK, BLOCK), 0)
                col = lax.broadcasted_iota(jnp.int32, (BLOCK, BLOCK), 1)
                keep = keep & (col <= row)
            bias[:, at - begin:at - begin + BLOCK] = jnp.where(keep, 0.0, -1e30).astype(F32)

        def head(h, carry):
            columns = pl.ds(pl.multiple_of(h * HEAD, HEAD), HEAD)
            scores = lax.dot_general(
                query[first:last, columns], keyval[0, begin:last, :],
                (((1,), (1,)), ((), ())), preferred_element_type=F32,
            )
            scores = scores * scale + bias[:, :width]
            peak = jnp.max(scores, axis=1, keepdims=True)
            expo = jnp.exp2(scores - peak).astype(BF16)
            out = jnp.dot(expo, values[begin:last, :], preferred_element_type=F32)
            attended[first:last, columns] = (out[:, :HEAD] / out[:, HEAD:]).astype(BF16)
            return carry

        lax.fori_loop(0, query.shape[1] // HEAD, head, 0)

    attend(3)
    attend(2)

    loads[2].wait()
    base = start[rows_of(mine), :].astype(F32)

    def add(k, total):
        place = (mine - k + GROUP) % GROUP
        arrived(reduce_buf, reduce_r, place)
        return total + (base - reduce_buf[place].astype(F32))

    partial = lax.fori_loop(1, GROUP, add, base - layer[rows_of(mine), :].astype(F32), unroll=True)
    twin_buf[twin] = partial.astype(BF16)
    each(TWINS, lambda k: twin_copy(k).start())

    each(COLUMN, lambda k: arrived(mom_all.at[sheet], momone_r, (column + k) % COLUMN))
    each(SHEET, lambda k: momtwo_copy(k).start())

    attend(1)
    attend(0)
    attended_out = pltpu.make_async_copy(attended, attended_hbm.at[0], local_sem.at[6])
    attended_out.start()

    each(TWINS, lambda k: arrived(twin_buf, twin_r, (twin + k) % TWINS))
    total = twin_buf[0].astype(F32)
    for t in range(1, TWINS):
        total = total + twin_buf[t].astype(F32)
    total = total * (1.0 / REPLICAS)
    average[mine] = total.astype(BF16)
    square = total * total
    parts = square[0:8, 0:128]
    for r in range(0, ROWS, 8):
        for c in range(0, square.shape[1], 128):
            if r or c:
                parts = parts + square[r:r + 8, c:c + 128]
    sum_one[plane] = parts
    each(PLANE, lambda k: sumone_copy(k).start())
    each(GROUP, lambda k: gather_copy(k).start())

    each(PLANE, lambda k: arrived(sum_one, sumone_r, (plane - k + PLANE) % PLANE))
    parts = sum_one[0]
    for p in range(1, PLANE):
        parts = parts + sum_one[p]
    sum_two[line] = parts
    each(LINE, lambda k: sumtwo_copy(k).start())

    each(SHEET, lambda k: arrived(mom_all, momtwo_r, (sheet - k + SHEET) % SHEET))
    for p in range(SHEET):
        for z in range(COLUMN):
            piece[:, :fold] = mom_all[p, z].astype(F32)
            at = ((p // 2) * 16 + z * 2 + p % 2) * 4
            for j in range(4):
                mom_full[at:at + 4, j * fold:(j + 1) * fold] = piece[4 * j:4 * j + 4, :fold]

    each(GROUP, lambda k: arrived(average, gather_r, (mine - k + GROUP) % GROUP))
    each(LINE, lambda k: arrived(sum_two, sumtwo_r, (line - k + LINE) % LINE))
    parts = sum_two[0]
    for y in range(1, LINE):
        parts = parts + sum_two[y]
    square = jnp.sum(jnp.sum(parts, axis=1, keepdims=True), axis=0, keepdims=True)
    factor = lax.rsqrt(square * (1.0 / (FRAG * D)) + 1e-06)

    def update(c, carry):
        rows = rows_of(c)
        grad = average[c].astype(F32) * factor
        moved = 0.9 * mom_full[rows, :] + grad
        fresh = (start[rows, :].astype(F32) - 0.7 * (grad + 0.9 * moved)).astype(BF16)
        blended[rows, :] = (0.5 * layer[rows, :].astype(F32) + 0.5 * fresh.astype(F32)).astype(BF16)
        return carry

    outs = []
    for part in range(2):
        lax.fori_loop(part * GROUP // 2, (part + 1) * GROUP // 2, update, 0, unroll=True)
        span = pl.ds(part * ROWS * GROUP // 2, ROWS * GROUP // 2)
        outs.append(pltpu.make_async_copy(blended.at[span], blended_hbm.at[0, span], local_sem.at[7 + part]))
        outs[-1].start()

    piece[...] = average[replica // 4].astype(F32)
    own = piece[0:4, :]
    for t in range(1, 4):
        own = jnp.where(low == t, piece[4 * t:4 * t + 4, :], own)
    newmom[...] = 0.9 * moment[...] + own * factor
    outs.append(pltpu.make_async_copy(newmom, newmom_hbm, local_sem.at[9]))
    outs[-1].start()

    each(GROUP, lambda k: reduce_copy(k).wait_send())
    each(TWINS, lambda k: twin_copy(k).wait_send())
    each(GROUP, lambda k: gather_copy(k).wait_send())
    each(COLUMN, lambda k: momone_copy(k).wait_send())
    each(SHEET, lambda k: momtwo_copy(k).wait_send())
    each(PLANE, lambda k: sumone_copy(k).wait_send())
    each(LINE, lambda k: sumtwo_copy(k).wait_send())
    attended_out.wait()
    for out in outs:
        out.wait()


def settle(newmom_in, blended_in, attended_in, newmom_out, blended_out, attended_out, newmom, blended, attended, sem):
    pieces = [(newmom_in, newmom, newmom_out)]
    for source, stage, target in ((attended_in, attended, attended_out), (blended_in, blended, blended_out)):
        for at in range(0, source.shape[1], 256):
            span = pl.ds(at, 256)
            pieces.append((source.at[0, span], stage.at[span], target.at[0, span]))
    into = [pltpu.make_async_copy(p[0], p[1], sem.at[0, i]) for i, p in enumerate(pieces)]
    out = [pltpu.make_async_copy(p[1], p[2], sem.at[1, i]) for i, p in enumerate(pieces)]
    for copy in into:
        copy.start()
    for i in range(len(pieces)):
        into[i].wait()
        out[i].start()
    for copy in out:
        copy.wait()


def shards(global_start, local_params, layer_index, momentum, queries, keyvals, segment_ids):
    rows, columns = global_start.shape
    length, width = queries.shape[1:]
    far = pl.BlockSpec(memory_space=pl.ANY)
    dma = pltpu.SemaphoreType.DMA
    out_shape = (
        jax.ShapeDtypeStruct(momentum.shape, F32),
        jax.ShapeDtypeStruct((1, rows, columns), BF16),
        jax.ShapeDtypeStruct(queries.shape, BF16),
    )
    results = pl.pallas_call(
        fused,
        out_shape=out_shape,
        in_specs=[far, far, far, far, far, far, far],
        out_specs=(far, far, far),
        scratch_shapes=[
            pltpu.VMEM(momentum.shape, F32),
            pltpu.VMEM((rows, columns), BF16),
            pltpu.VMEM((length, width), BF16),
            pltpu.SMEM((1,), jnp.int32),
            pltpu.VMEM((rows, columns), BF16),
            pltpu.VMEM(local_params.shape[1:], BF16),
            pltpu.VMEM((rows, columns), BF16),
            pltpu.VMEM(momentum.shape, F32),
            pltpu.VMEM((length, width), BF16),
            pltpu.VMEM(keyvals.shape[1:], BF16),
            pltpu.VMEM((1, length), jnp.int32),
            pltpu.VMEM((length, 2 * HEAD), BF16),
            pltpu.VMEM((BLOCK, BLOCK + SPAN), F32),
            pltpu.VMEM((GROUP, ROWS, columns), BF16),
            pltpu.VMEM((TWINS, ROWS, columns), BF16),
            pltpu.VMEM((GROUP, ROWS, columns), BF16),
            pltpu.VMEM((SHEET, COLUMN, ROWS, columns // 4), BF16),
            pltpu.VMEM((rows, columns), F32),
            pltpu.VMEM((ROWS, columns), F32),
            pltpu.VMEM((PLANE, 8, 128), F32),
            pltpu.VMEM((LINE, 8, 128), F32),
            dma((11,)),
            dma((GROUP,)), dma((GROUP,)),
            dma((TWINS,)), dma((TWINS,)),
            dma((GROUP,)), dma((GROUP,)),
            dma((COLUMN,)), dma((COLUMN,)),
            dma((SHEET,)), dma((SHEET,)),
            dma((PLANE,)), dma((PLANE,)),
            dma((LINE,)), dma((LINE,)),
        ],
        compiler_params=pltpu.CompilerParams(
            collective_id=0, has_side_effects=True, vmem_limit_bytes=56 * 1024 * 1024
        ),
    )(global_start, local_params, layer_index, momentum, queries, keyvals, segment_ids)
    return pl.pallas_call(
        settle,
        out_shape=out_shape,
        in_specs=[far] * 3,
        out_specs=(far,) * 3,
        scratch_shapes=[
            pltpu.VMEM(momentum.shape, F32),
            pltpu.VMEM((rows, columns), BF16),
            pltpu.VMEM((length, width), BF16),
            dma((2, 6)),
        ],
        compiler_params=pltpu.CompilerParams(vmem_limit_bytes=60 * 1024 * 1024),
    )(*results)


def solution(mesh):
    in_specs = (
        P(None, "tensor"),
        P("replica", None, None, "tensor"),
        P("replica"),
        P("replica", "tensor"),
        P("replica", None, "tensor"),
        P("replica", None, None, "tensor"),
        P("replica", None),
    )
    out_specs = (P("replica", "tensor"), P("replica", None, "tensor"), P("replica", None, "tensor"))
    return jax.shard_map(shards, mesh=mesh, in_specs=in_specs, out_specs=out_specs, check_vma=False)
```

time: 53.5 us -> 46.5 us (0.87)
  the two profiles are of different devices: /device:TPU:8 before, /device:TPU:1 now
where the time goes in v2:
time: 46.5 us; the launch traced here: 46.3 us
  Pallas kernels  45 us (97%)
  between operations  1.29 us (3%)
    pallas_call x1, Pallas kernels, shards(): pl.pallas_call(fused, out_shape=out_shape, in_specs=[far, far, far, far,...  42.7 us
    pallas_call x1, Pallas kernels, shards(): pl.pallas_call(settle, out_shape=out_shape, in_specs=[far] * 3, out_specs...  2.27 us

profile of v2, /device:TPU:1, one launch (start us, length us, event | category | flops | bytes accessed | tf_op | source)
XLA Modules:
  0.0 46.3 jit_solution(5235455107253811880)
XLA Ops:
  1.3 42.7 %shard_map.94 = (f32[4,1024]{1,0:T(4,128)}, bf16[1,256,1024]{2,1,0:T(8,128)(2,1)}, bf16[1,1024,512]{2,1,0:T(8,128)(2,1)}) custom-call(bf16[256,1024]{1,0:T(8,128)(2,1)} %start_hbm.1, bf16[1,2,256,1024]{3,2,1,0:T(8,128)(2,1)} %params_hbm.1, s32[1]{0:T(128)S(6)} %copy.10.slot_hbm, f32[4,1024]{1,0:T(4,128)} %moment_hbm.1, bf16[1,1024,512]{2,1,0:T(8,128)(2,1)} %query_hbm.1, ...), custom_call_target="tpu_custom_call" | custom-call | tf_op jit(solution)/shard_map/pallas_call | solution.py:309
  44.0 2.3 %shard_map.95 = (f32[4,1024]{1,0:T(4,128)}, bf16[1,256,1024]{2,1,0:T(8,128)(2,1)}, bf16[1,1024,512]{2,1,0:T(8,128)(2,1)}) custom-call(f32[4,1024]{1,0:T(4,128)} %get-tuple-element.6.newmom_in, bf16[1,256,1024]{2,1,0:T(8,128)(2,1)} %get-tuple-element.7.blended_in, bf16[1,1024,512]{2,1,0:T(8,128)(2,1)} %get-tuple-element.8.attended_in), custom_call_target="tpu_custom_call" | custom-call | tf_op jit(solution)/shard_map/pallas_call | solution.py:349

commit v3 on v2

--- a/solution.py
+++ b/solution.py
@@ -19,6 +19,10 @@
 BLOCK = 256
 HEAD = 128
 SPAN = 512
+FAR16 = (11, 10, 9, 15, 7, 8, 14, 13, 6, 5, 3, 12, 4, 2, 1)
+FAR8 = (4, 3, 5, 2, 6, 1, 7)
+FAR4 = (2, 1, 3)
+SHEETS = (5, 4, 7, 3, 6, 2, 1)
 F32 = jnp.float32
 BF16 = jnp.bfloat16
 
@@ -27,7 +31,7 @@
     start_hbm, params_hbm, slot_hbm, moment_hbm, query_hbm, keyval_hbm, segment_hbm,
     newmom_hbm, blended_hbm, attended_hbm,
     newmom, blended, attended, slot_ref, start, params, layer, moment, query, keyval, segment, values, bias,
-    reduce_buf, twin_buf, average, mom_all, mom_full, piece, sum_one, sum_two,
+    reduce_buf, twin_buf, average, mom_all, base_full, piece, sum_one, sum_two,
     local_sem, reduce_s, reduce_r, twin_s, twin_r, gather_s, gather_r,
     momone_s, momone_r, momtwo_s, momtwo_r, sumone_s, sumone_r, sumtwo_s, sumtwo_r,
 ):
@@ -68,14 +72,14 @@
         )
 
     def reduce_copy(k):
-        to = (mine + k) % GROUP
+        to = off16(mine, k)
         return remote(layer.at[rows_of(to)], reduce_buf.at[mine], reduce_s.at[k], reduce_r.at[mine], member(to))
 
     def twin_copy(k):
         return remote(twin_buf.at[twin], twin_buf.at[twin], twin_s.at[k], twin_r.at[twin], twin_of((twin + k) % TWINS))
 
     def gather_copy(k):
-        return remote(average.at[mine], average.at[mine], gather_s.at[k], gather_r.at[mine], member((mine + k) % GROUP))
+        return remote(average.at[mine], average.at[mine], gather_s.at[k], gather_r.at[mine], member(off16(mine, k)))
 
     def momone_copy(k):
         return remote(
@@ -85,24 +89,34 @@
 
     def momtwo_copy(k):
         return remote(
-            mom_all.at[sheet], mom_all.at[sheet], momtwo_s.at[k], momtwo_r.at[sheet], sheet_of((sheet + k) % SHEET)
+            mom_all.at[sheet], mom_all.at[sheet], momtwo_s.at[k], momtwo_r.at[sheet], sheet_of(off_sheet(sheet, k))
         )
 
     def sumone_copy(k):
         return remote(
-            sum_one.at[plane], sum_one.at[plane], sumone_s.at[k], sumone_r.at[plane], plane_of((plane + k) % PLANE)
+            sum_one.at[line], sum_one.at[line], sumone_s.at[k], sumone_r.at[line], line_of((line + k) % LINE)
         )
 
     def sumtwo_copy(k):
         return remote(
-            sum_two.at[line], sum_two.at[line], sumtwo_s.at[k], sumtwo_r.at[line], line_of((line + k) % LINE)
-        )
-
-    def each(count, act):
-        def step(k, carry):
+            sum_two.at[plane], sum_two.at[plane], sumtwo_s.at[k], sumtwo_r.at[plane], plane_of(off16(plane, k))
+        )
+
+    def each(order, act):
+        for k in order:
             act(k)
-            return carry
-        lax.fori_loop(1, count, step, 0, unroll=True)
+
+    def off16(place, k):
+        return (place // 4 + k // 4) % 4 * 4 + (place // 2 + k // 2) % 2 * 2 + (place + k) % 2
+
+    def back16(place, k):
+        return (place // 4 + 4 - k // 4) % 4 * 4 + (place // 2 + k // 2) % 2 * 2 + (place + k) % 2
+
+    def off_sheet(place, k):
+        return (place // 2 + k // 2) % 4 * 2 + (place + k) % 2
+
+    def back_sheet(place, k):
+        return (place // 2 + 4 - k // 2) % 4 * 2 + (place + k) % 2
 
     def arrived(slots, sems, slot):
         pltpu.make_async_copy(slots.at[slot], slots.at[slot], sems.at[slot]).wait()
@@ -115,22 +129,21 @@
         pltpu.make_async_copy(keyval_hbm.at[0], keyval, local_sem.at[4]),
         pltpu.make_async_copy(query_hbm.at[0], query, local_sem.at[5]),
     ]
+    barrier = pltpu.get_barrier_semaphore()
+
+    def greet(device):
+        pl.semaphore_signal(barrier, inc=1, device_id=device, device_id_type=MESH)
+
+    each(FAR16, lambda k: greet(member(off16(mine, k))))
     loads[0].start()
     index = pltpu.make_async_copy(slot_hbm, slot_ref, local_sem.at[10])
     index.start()
-
-    barrier = pltpu.get_barrier_semaphore()
-
-    def greet(device):
-        pl.semaphore_signal(barrier, inc=1, device_id=device, device_id_type=MESH)
-
-    each(GROUP, lambda k: greet(member((mine + k) % GROUP)))
-    each(COLUMN // 2, lambda k: greet(column_of((column + 2 * k) % COLUMN)))
-    each(COLUMN // 2, lambda k: greet(column_of((column + 2 * k) % COLUMN // 2 * 2 + 1 - column % 2)))
+    each(FAR4, lambda k: greet(column_of((column + 2 * k) % COLUMN)))
+    each(FAR4, lambda k: greet(column_of((column + 2 * k) % COLUMN // 2 * 2 + 1 - column % 2)))
     for p in range(0, PLANE, 2):
         greet(plane_of(p + 1 - tensor % 2))
-    each(LINE // 2, lambda k: greet(line_of((line + 2 * k) % LINE)))
-    each(LINE // 2, lambda k: greet(line_of((line + 2 * k) % LINE // 2 * 2 + 1 - line % 2)))
+    each(FAR4, lambda k: greet(line_of((line + 2 * k) % LINE)))
+    each(FAR4, lambda k: greet(line_of((line + 2 * k) % LINE // 2 * 2 + 1 - line % 2)))
     for load in loads[1:]:
         load.start()
 
@@ -145,9 +158,9 @@
     mom_all[sheet, column] = piece[:, :fold].astype(BF16)
     pl.semaphore_wait(barrier, GROUP + COLUMN + PLANE // 2 + LINE - 5)
 
-    each(COLUMN, lambda k: momone_copy(k).start())
-
-    each(GROUP, lambda k: reduce_copy(k).start())
+    each(FAR8, lambda k: momone_copy(k).start())
+
+    each(FAR16, lambda k: reduce_copy(k).start())
     for load in loads[3:]:
         load.wait()
     values[:, :HEAD] = keyval[1]
@@ -188,24 +201,23 @@
     loads[2].wait()
     base = start[rows_of(mine), :].astype(F32)
 
-    def add(k, total):
-        place = (mine - k + GROUP) % GROUP
+    partial = base - layer[rows_of(mine), :].astype(F32)
+    for k in FAR16:
+        place = back16(mine, k)
         arrived(reduce_buf, reduce_r, place)
-        return total + (base - reduce_buf[place].astype(F32))
-
-    partial = lax.fori_loop(1, GROUP, add, base - layer[rows_of(mine), :].astype(F32), unroll=True)
+        partial = partial + (base - reduce_buf[place].astype(F32))
     twin_buf[twin] = partial.astype(BF16)
-    each(TWINS, lambda k: twin_copy(k).start())
-
-    each(COLUMN, lambda k: arrived(mom_all.at[sheet], momone_r, (column + k) % COLUMN))
-    each(SHEET, lambda k: momtwo_copy(k).start())
+    each(FAR4, lambda k: twin_copy(k).start())
+
+    each(FAR8, lambda k: arrived(mom_all.at[sheet], momone_r, (column - k + COLUMN) % COLUMN))
+    each(SHEETS, lambda k: momtwo_copy(k).start())
 
     attend(1)
     attend(0)
     attended_out = pltpu.make_async_copy(attended, attended_hbm.at[0], local_sem.at[6])
     attended_out.start()
 
-    each(TWINS, lambda k: arrived(twin_buf, twin_r, (twin + k) % TWINS))
+    each(FAR4, lambda k: arrived(twin_buf, twin_r, (twin + TWINS - k) % TWINS))
     total = twin_buf[0].astype(F32)
     for t in range(1, TWINS):
         total = total + twin_buf[t].astype(F32)
@@ -217,39 +229,51 @@
         for c in range(0, square.shape[1], 128):
             if r or c:
                 parts = parts + square[r:r + 8, c:c + 128]
-    sum_one[plane] = parts
-    each(PLANE, lambda k: sumone_copy(k).start())
-    each(GROUP, lambda k: gather_copy(k).start())
-
-    each(PLANE, lambda k: arrived(sum_one, sumone_r, (plane - k + PLANE) % PLANE))
+    sum_one[line] = jnp.sum(parts, axis=0, keepdims=True)
+    each(FAR8, lambda k: sumone_copy(k).start())
+    each(FAR16, lambda k: gather_copy(k).start())
+
+    each(FAR8, lambda k: arrived(sum_one, sumone_r, (line - k + LINE) % LINE))
     parts = sum_one[0]
-    for p in range(1, PLANE):
-        parts = parts + sum_one[p]
-    sum_two[line] = parts
-    each(LINE, lambda k: sumtwo_copy(k).start())
-
-    each(SHEET, lambda k: arrived(mom_all, momtwo_r, (sheet - k + SHEET) % SHEET))
+    for y in range(1, LINE):
+        parts = parts + sum_one[y]
+    sum_two[plane] = parts
+    each(FAR16, lambda k: sumtwo_copy(k).start())
+
+    each(SHEETS, lambda k: arrived(mom_all, momtwo_r, back_sheet(sheet, k)))
     for p in range(SHEET):
         for z in range(COLUMN):
             piece[:, :fold] = mom_all[p, z].astype(F32)
             at = ((p // 2) * 16 + z * 2 + p % 2) * 4
             for j in range(4):
-                mom_full[at:at + 4, j * fold:(j + 1) * fold] = piece[4 * j:4 * j + 4, :fold]
-
-    each(GROUP, lambda k: arrived(average, gather_r, (mine - k + GROUP) % GROUP))
-    each(LINE, lambda k: arrived(sum_two, sumtwo_r, (line - k + LINE) % LINE))
+                base_full[at:at + 4, j * fold:(j + 1) * fold] = piece[4 * j:4 * j + 4, :fold]
+
+    def ahead(c, carry):
+        rows = rows_of(c)
+        base_full[rows, :] = start[rows, :].astype(F32) - (0.7 * 0.9 * 0.9) * base_full[rows, :]
+        return carry
+
+    lax.fori_loop(0, GROUP, ahead, 0)
+
+    each(FAR16, lambda k: reduce_copy(k).wait_send())
+    each(FAR4, lambda k: twin_copy(k).wait_send())
+    each(FAR16, lambda k: gather_copy(k).wait_send())
+    each(FAR8, lambda k: momone_copy(k).wait_send())
+    each(SHEETS, lambda k: momtwo_copy(k).wait_send())
+    each(FAR8, lambda k: sumone_copy(k).wait_send())
+    each(FAR16, lambda k: arrived(average, gather_r, back16(mine, k)))
+    each(FAR16, lambda k: arrived(sum_two, sumtwo_r, back16(plane, k)))
     parts = sum_two[0]
-    for y in range(1, LINE):
-        parts = parts + sum_two[y]
-    square = jnp.sum(jnp.sum(parts, axis=1, keepdims=True), axis=0, keepdims=True)
+    for p in range(1, PLANE):
+        parts = parts + sum_two[p]
+    square = jnp.sum(parts, axis=1, keepdims=True)
     factor = lax.rsqrt(square * (1.0 / (FRAG * D)) + 1e-06)
+    step = factor * (0.7 * 1.9)
 
     def update(c, carry):
         rows = rows_of(c)
-        grad = average[c].astype(F32) * factor
-        moved = 0.9 * mom_full[rows, :] + grad
-        fresh = (start[rows, :].astype(F32) - 0.7 * (grad + 0.9 * moved)).astype(BF16)
-        blended[rows, :] = (0.5 * layer[rows, :].astype(F32) + 0.5 * fresh.astype(F32)).astype(BF16)
+        fresh = (base_full[rows, :] - average[c].astype(F32) * step).astype(BF16)
+        blended[rows, :] = (0.5 * (layer[rows, :].astype(F32) + fresh.astype(F32))).astype(BF16)
         return carry
 
     outs = []
@@ -267,13 +291,7 @@
     outs.append(pltpu.make_async_copy(newmom, newmom_hbm, local_sem.at[9]))
     outs[-1].start()
 
-    each(GROUP, lambda k: reduce_copy(k).wait_send())
-    each(TWINS, lambda k: twin_copy(k).wait_send())
-    each(GROUP, lambda k: gather_copy(k).wait_send())
-    each(COLUMN, lambda k: momone_copy(k).wait_send())
-    each(SHEET, lambda k: momtwo_copy(k).wait_send())
-    each(PLANE, lambda k: sumone_copy(k).wait_send())
-    each(LINE, lambda k: sumtwo_copy(k).wait_send())
+    each(FAR16, lambda k: sumtwo_copy(k).wait_send())
     attended_out.wait()
     for out in outs:
         out.wait()
@@ -331,16 +349,16 @@
             pltpu.VMEM((SHEET, COLUMN, ROWS, columns // 4), BF16),
             pltpu.VMEM((rows, columns), F32),
             pltpu.VMEM((ROWS, columns), F32),
-            pltpu.VMEM((PLANE, 8, 128), F32),
-            pltpu.VMEM((LINE, 8, 128), F32),
+            pltpu.VMEM((LINE, 1, 128), F32),
+            pltpu.VMEM((PLANE, 1, 128), F32),
             dma((11,)),
             dma((GROUP,)), dma((GROUP,)),
             dma((TWINS,)), dma((TWINS,)),
             dma((GROUP,)), dma((GROUP,)),
             dma((COLUMN,)), dma((COLUMN,)),
             dma((SHEET,)), dma((SHEET,)),
+            dma((LINE,)), dma((LINE,)),
             dma((PLANE,)), dma((PLANE,)),
-            dma((LINE,)), dma((LINE,)),
         ],
         compiler_params=pltpu.CompilerParams(
             collective_id=0, has_side_effects=True, vmem_limit_bytes=56 * 1024 * 1024

time: 46.5 us -> 44.3 us (0.953)
  Pallas kernels: 45 us -> 42.8 us
    pallas_call x1, Pallas kernels: 42.7 us -> 40.5 us  [shards(): pl.pallas_call(fused, out_shape=out_shape, in_specs=[far, far, far, far,...]
where the time goes in v3:
time: 44.3 us; the launch traced here: 44.1 us
  Pallas kernels  42.8 us (97%)
  between operations  1.29 us (3%)
    pallas_call x1, Pallas kernels, shards(): pl.pallas_call(fused, out_shape=out_shape, in_specs=[far, far, far, far,...  40.5 us
    pallas_call x1, Pallas kernels, shards(): pl.pallas_call(settle, out_shape=out_shape, in_specs=[far] * 3, out_specs...  2.27 us

profile of v3, /device:TPU:1, one launch (start us, length us, event | category | flops | bytes accessed | tf_op | source)
XLA Modules:
  0.0 44.1 jit_solution(1163762060535125338)
XLA Ops:
  1.3 40.5 %shard_map.94 = (f32[4,1024]{1,0:T(4,128)}, bf16[1,256,1024]{2,1,0:T(8,128)(2,1)}, bf16[1,1024,512]{2,1,0:T(8,128)(2,1)}) custom-call(bf16[256,1024]{1,0:T(8,128)(2,1)} %start_hbm.1, bf16[1,2,256,1024]{3,2,1,0:T(8,128)(2,1)} %params_hbm.1, s32[1]{0:T(128)S(6)} %copy.10.slot_hbm, f32[4,1024]{1,0:T(4,128)} %moment_hbm.1, bf16[1,1024,512]{2,1,0:T(8,128)(2,1)} %query_hbm.1, ...), custom_call_target="tpu_custom_call" | custom-call | tf_op jit(solution)/shard_map/pallas_call | solution.py:327
  41.8 2.3 %shard_map.95 = (f32[4,1024]{1,0:T(4,128)}, bf16[1,256,1024]{2,1,0:T(8,128)(2,1)}, bf16[1,1024,512]{2,1,0:T(8,128)(2,1)}) custom-call(f32[4,1024]{1,0:T(4,128)} %get-tuple-element.6.newmom_in, bf16[1,256,1024]{2,1,0:T(8,128)(2,1)} %get-tuple-element.7.blended_in, bf16[1,1024,512]{2,1,0:T(8,128)(2,1)} %get-tuple-element.8.attended_in), custom_call_target="tpu_custom_call" | custom-call | tf_op jit(solution)/shard_map/pallas_call | solution.py:367

commit v4 on v3

--- a/solution.py
+++ b/solution.py
@@ -37,30 +37,54 @@
 ):
     replica = lax.axis_index("replica")
     tensor = lax.axis_index("tensor")
-    xs, twin, low = replica // 16, (replica // 4) % TWINS, replica % 4
+    xs, twin, low = lax.div(replica, 16), lax.rem(lax.div(replica, 4), TWINS), lax.rem(replica, 4)
+    zl, yl = lax.div(low, 2), lax.rem(low, 2)
+    yh, core = lax.div(tensor, 2), lax.rem(tensor, 2)
     mine = xs * 4 + low
-    plane = (replica // 16) * 4 + ((replica // 2) % 2) * 2 + tensor % 2
-    line = (tensor // 2) * 2 + replica % 2
-    column = (replica // 2) % COLUMN
-    sheet = xs * 2 + replica % 2
-
-    def member(g):
-        return ((g // 4) * 16 + twin * 4 + g % 4, tensor)
-
-    def twin_of(t):
-        return (xs * 16 + t * 4 + low, tensor)
-
-    def plane_of(p):
-        return ((p // 4) * 16 + twin * 4 + ((p // 2) % 2) * 2 + replica % 2, (tensor // 2) * 2 + p % 2)
-
-    def line_of(y):
-        return ((replica // 2) * 2 + y % 2, (y // 2) * 2 + tensor % 2)
-
-    def column_of(z):
-        return (xs * 16 + z * 2 + replica % 2, tensor)
-
-    def sheet_of(p):
-        return ((p // 2) * 16 + column * 2 + p % 2, tensor)
+    plane = xs * 4 + zl * 2 + core
+    line = yh * 2 + yl
+    column = twin * 2 + zl
+    sheet = xs * 2 + yl
+
+    x_at = [xs] + [lax.rem(xs + d, 4) for d in (1, 2, 3)]
+    z_at, y_at, core_at = (zl * 2, 2 - zl * 2), (yl, 1 - yl), (core, 1 - core)
+    twin_at = [twin] + [lax.rem(twin + d, TWINS) for d in (1, 2, 3)]
+    column_at = [column] + [lax.rem(column + d, COLUMN) for d in range(1, COLUMN)]
+    line_at = [line] + [lax.rem(line + d, LINE) for d in range(1, LINE)]
+    x_four, x_two = [x * 4 for x in x_at], [x * 2 for x in x_at]
+    x_member = [x * 16 + twin * 4 for x in x_at]
+    x_sheet = [x * 16 + column * 2 for x in x_at]
+    rest = replica - yl
+
+    def off16(k):
+        return x_four[k // 4] + (z_at[k // 2 % 2] + y_at[k % 2])
+
+    def off_plane(k):
+        return x_four[k // 4] + (z_at[k // 2 % 2] + core_at[k % 2])
+
+    def off_sheet(k):
+        return x_two[k // 2] + y_at[k % 2]
+
+    def back(k, pair):
+        return (4 - k // pair) % 4 * pair + k % pair
+
+    def member(k):
+        return (x_member[k // 4] + (z_at[k // 2 % 2] + y_at[k % 2]), tensor)
+
+    def twin_of(k):
+        return (xs * 16 + low + twin_at[k] * 4, tensor)
+
+    def plane_of(k):
+        return (x_member[k // 4] + (z_at[k // 2 % 2] + yl), yh * 2 + core_at[k % 2])
+
+    def line_of(k):
+        return (rest + lax.rem(line_at[k], 2), line_at[k] - lax.rem(line_at[k], 2) + core)
+
+    def column_of(k):
+        return (xs * 16 + yl + column_at[k] * 2, tensor)
+
+    def sheet_of(k):
+        return (x_sheet[k // 2] + y_at[k % 2], tensor)
 
     def rows_of(g):
         return pl.ds(pl.multiple_of(g * ROWS, ROWS), ROWS)
@@ -72,51 +96,30 @@
         )
 
     def reduce_copy(k):
-        to = off16(mine, k)
-        return remote(layer.at[rows_of(to)], reduce_buf.at[mine], reduce_s.at[k], reduce_r.at[mine], member(to))
+        return remote(layer.at[rows_of(off16(k))], reduce_buf.at[mine], reduce_s.at[k], reduce_r.at[mine], member(k))
 
     def twin_copy(k):
-        return remote(twin_buf.at[twin], twin_buf.at[twin], twin_s.at[k], twin_r.at[twin], twin_of((twin + k) % TWINS))
+        return remote(twin_buf.at[twin], twin_buf.at[twin], twin_s.at[k], twin_r.at[twin], twin_of(k))
 
     def gather_copy(k):
-        return remote(average.at[mine], average.at[mine], gather_s.at[k], gather_r.at[mine], member(off16(mine, k)))
+        return remote(average.at[mine], average.at[mine], gather_s.at[k], gather_r.at[mine], member(k))
 
     def momone_copy(k):
-        return remote(
-            mom_all.at[sheet, column], mom_all.at[sheet, column], momone_s.at[k], momone_r.at[column],
-            column_of((column + k) % COLUMN),
-        )
+        own = mom_all.at[sheet, column]
+        return remote(own, own, momone_s.at[k], momone_r.at[column], column_of(k))
 
     def momtwo_copy(k):
-        return remote(
-            mom_all.at[sheet], mom_all.at[sheet], momtwo_s.at[k], momtwo_r.at[sheet], sheet_of(off_sheet(sheet, k))
-        )
+        return remote(mom_all.at[sheet], mom_all.at[sheet], momtwo_s.at[k], momtwo_r.at[sheet], sheet_of(k))
 
     def sumone_copy(k):
-        return remote(
-            sum_one.at[line], sum_one.at[line], sumone_s.at[k], sumone_r.at[line], line_of((line + k) % LINE)
-        )
+        return remote(sum_one.at[line], sum_one.at[line], sumone_s.at[k], sumone_r.at[line], line_of(k))
 
     def sumtwo_copy(k):
-        return remote(
-            sum_two.at[plane], sum_two.at[plane], sumtwo_s.at[k], sumtwo_r.at[plane], plane_of(off16(plane, k))
-        )
+        return remote(sum_two.at[plane], sum_two.at[plane], sumtwo_s.at[k], sumtwo_r.at[plane], plane_of(k))
 
     def each(order, act):
         for k in order:
             act(k)
-
-    def off16(place, k):
-        return (place // 4 + k // 4) % 4 * 4 + (place // 2 + k // 2) % 2 * 2 + (place + k) % 2
-
-    def back16(place, k):
-        return (place // 4 + 4 - k // 4) % 4 * 4 + (place // 2 + k // 2) % 2 * 2 + (place + k) % 2
-
-    def off_sheet(place, k):
-        return (place // 2 + k // 2) % 4 * 2 + (place + k) % 2
-
-    def back_sheet(place, k):
-        return (place // 2 + 4 - k // 2) % 4 * 2 + (place + k) % 2
 
     def arrived(slots, sems, slot):
         pltpu.make_async_copy(slots.at[slot], slots.at[slot], sems.at[slot]).wait()
@@ -134,16 +137,18 @@
     def greet(device):
         pl.semaphore_signal(barrier, inc=1, device_id=device, device_id_type=MESH)
 
-    each(FAR16, lambda k: greet(member(off16(mine, k))))
+    each(FAR16, lambda k: greet(member(k)))
     loads[0].start()
     index = pltpu.make_async_copy(slot_hbm, slot_ref, local_sem.at[10])
     index.start()
-    each(FAR4, lambda k: greet(column_of((column + 2 * k) % COLUMN)))
-    each(FAR4, lambda k: greet(column_of((column + 2 * k) % COLUMN // 2 * 2 + 1 - column % 2)))
-    for p in range(0, PLANE, 2):
-        greet(plane_of(p + 1 - tensor % 2))
-    each(FAR4, lambda k: greet(line_of((line + 2 * k) % LINE)))
-    each(FAR4, lambda k: greet(line_of((line + 2 * k) % LINE // 2 * 2 + 1 - line % 2)))
+    for k in FAR8:
+        if k % 2 == 0:
+            greet(column_of(k))
+            greet(line_of(k))
+    for d in (1, 2, 3):
+        greet((xs * 16 + yl + twin_at[d] * 4 + z_at[1], tensor))
+        greet((rest + y_at[1], lax.rem(yh + d, 4) * 2 + core))
+    each(range(1, 16, 2), lambda k: greet(plane_of(k)))
     for load in loads[1:]:
         load.start()
 
@@ -203,13 +208,13 @@
 
     partial = base - layer[rows_of(mine), :].astype(F32)
     for k in FAR16:
-        place = back16(mine, k)
+        place = off16(back(k, 4))
         arrived(reduce_buf, reduce_r, place)
         partial = partial + (base - reduce_buf[place].astype(F32))
     twin_buf[twin] = partial.astype(BF16)
     each(FAR4, lambda k: twin_copy(k).start())
 
-    each(FAR8, lambda k: arrived(mom_all.at[sheet], momone_r, (column - k + COLUMN) % COLUMN))
+    each(FAR8, lambda k: arrived(mom_all.at[sheet], momone_r, column_at[COLUMN - k]))
     each(SHEETS, lambda k: momtwo_copy(k).start())
 
     attend(1)
@@ -217,7 +222,7 @@
     attended_out = pltpu.make_async_copy(attended, attended_hbm.at[0], local_sem.at[6])
     attended_out.start()
 
-    each(FAR4, lambda k: arrived(twin_buf, twin_r, (twin + TWINS - k) % TWINS))
+    each(FAR4, lambda k: arrived(twin_buf, twin_r, twin_at[TWINS - k]))
     total = twin_buf[0].astype(F32)
     for t in range(1, TWINS):
         total = total + twin_buf[t].astype(F32)
@@ -233,14 +238,14 @@
     each(FAR8, lambda k: sumone_copy(k).start())
     each(FAR16, lambda k: gather_copy(k).start())
 
-    each(FAR8, lambda k: arrived(sum_one, sumone_r, (line - k + LINE) % LINE))
+    each(FAR8, lambda k: arrived(sum_one, sumone_r, line_at[LINE - k]))
     parts = sum_one[0]
     for y in range(1, LINE):
         parts = parts + sum_one[y]
     sum_two[plane] = parts
     each(FAR16, lambda k: sumtwo_copy(k).start())
 
-    each(SHEETS, lambda k: arrived(mom_all, momtwo_r, back_sheet(sheet, k)))
+    each(SHEETS, lambda k: arrived(mom_all, momtwo_r, off_sheet(back(k, 2))))
     for p in range(SHEET):
         for z in range(COLUMN):
             piece[:, :fold] = mom_all[p, z].astype(F32)
@@ -261,8 +266,8 @@
     each(FAR8, lambda k: momone_copy(k).wait_send())
     each(SHEETS, lambda k: momtwo_copy(k).wait_send())
     each(FAR8, lambda k: sumone_copy(k).wait_send())
-    each(FAR16, lambda k: arrived(average, gather_r, back16(mine, k)))
-    each(FAR16, lambda k: arrived(sum_two, sumtwo_r, back16(plane, k)))
+    each(FAR16, lambda k: arrived(average, gather_r, off16(back(k, 4))))
+    each(FAR16, lambda k: arrived(sum_two, sumtwo_r, off_plane(back(k, 4))))
     parts = sum_two[0]
     for p in range(1, PLANE):
         parts = parts + sum_two[p]
@@ -283,7 +288,7 @@
         outs.append(pltpu.make_async_copy(blended.at[span], blended_hbm.at[0, span], local_sem.at[7 + part]))
         outs[-1].start()
 
-    piece[...] = average[replica // 4].astype(F32)
+    piece[...] = average[lax.div(replica, 4)].astype(F32)
     own = piece[0:4, :]
     for t in range(1, 4):
         own = jnp.where(low == t, piece[4 * t:4 * t + 4, :], own)

time: 44.3 us -> 44 us (level)
  no operation moved by 1% of the time
where the time goes in v4:
time: 44 us; the launch traced here: 43.8 us
  Pallas kernels  42.5 us (97%)
  between operations  1.29 us (3%)
    pallas_call x1, Pallas kernels, shards(): pl.pallas_call(fused, out_shape=out_shape, in_specs=[far, far, far, far,...  40.2 us
    pallas_call x1, Pallas kernels, shards(): pl.pallas_call(settle, out_shape=out_shape, in_specs=[far] * 3, out_specs...  2.27 us

profile of v4, /device:TPU:1, one launch (start us, length us, event | category | flops | bytes accessed | tf_op | source)
XLA Modules:
  0.0 43.8 jit_solution(3516029995166100785)
XLA Ops:
  1.3 40.2 %shard_map.94 = (f32[4,1024]{1,0:T(4,128)}, bf16[1,256,1024]{2,1,0:T(8,128)(2,1)}, bf16[1,1024,512]{2,1,0:T(8,128)(2,1)}) custom-call(bf16[256,1024]{1,0:T(8,128)(2,1)} %start_hbm.1, bf16[1,2,256,1024]{3,2,1,0:T(8,128)(2,1)} %params_hbm.1, s32[1]{0:T(128)S(6)} %copy.10.slot_hbm, f32[4,1024]{1,0:T(4,128)} %moment_hbm.1, bf16[1,1024,512]{2,1,0:T(8,128)(2,1)} %query_hbm.1, ...), custom_call_target="tpu_custom_call" | custom-call | tf_op jit(solution)/shard_map/pallas_call | solution.py:332
  41.5 2.3 %shard_map.95 = (f32[4,1024]{1,0:T(4,128)}, bf16[1,256,1024]{2,1,0:T(8,128)(2,1)}, bf16[1,1024,512]{2,1,0:T(8,128)(2,1)}) custom-call(f32[4,1024]{1,0:T(4,128)} %get-tuple-element.6.newmom_in, bf16[1,256,1024]{2,1,0:T(8,128)(2,1)} %get-tuple-element.7.blended_in, bf16[1,1024,512]{2,1,0:T(8,128)(2,1)} %get-tuple-element.8.attended_in), custom_call_target="tpu_custom_call" | custom-call | tf_op jit(solution)/shard_map/pallas_call | solution.py:372
